TPU v7x, 32 devices: a whole 2x2x4 slice. The times are simulated.
32 devices in a mesh: row: 4 (over y, x), col: 4 (over z), freq: 2 (over core).
Axes of the slice: x: 2, y: 2, z: 4, core: 2. Of those that a mesh axis runs over, the one named last changes fastest.
Arguments:
- visibility: bfloat16 [16, 8, 16, 64, 128], P(('row', 'col'), None, 'freq'), may hold values from -6 to 6
- tasks: int32 [16, 3], P(('row', 'col')), may hold values from 0 to 3, as said below
- flags: int32 [16, 256], P(None, ('row', 'col')), may hold values 0 or 1
- station_uvw: float32 [16, 3, 256], replicated, may hold values from -256 to 256
- comp_lm: float32 [2, 512], replicated, may hold values from -0.08 to 0.08
- intensity: float32 [512], replicated, may hold values from 0.02 to 0.2
- direction: int32 [512], replicated, may hold values from 0 to 7, as said below
- coefs: float32 [4, 2, 8, 256], P(None, None, None, ('row', 'col')), may hold values from -6 to 6
Outputs:
- gradient: float32 [4, 2, 8, 256], P(None, None, None, ('row', 'col'))
Inputs may be any that keep to these rules, and one draw needn't show every extreme that they name: Each row of tasks is (bi, bj, h) with bi <= bj: h is 0 or 1 when bi < bj and 2 when bi == bj; every pair bi < bj appears with h = 0 and with h = 1, and every block with h = 2, each exactly once, in an order drawn from the seed. Every direction holds exactly 64 components.
All inputs are finite; a program needn't handle non-finite values. No bound on the sum of `flags` on one device may be relied on, other than what follows from the above.
Results may differ from a plain program's by a relative error of at most 0.0003.
Values sent between devices are 32-bit elements; how exact they have to be, the bound alone decides.
A program may use at most 64 MiB of HBM per device.

v0:
```python
import math

import jax
import jax.numpy as jnp
from jax import lax
from jax.sharding import PartitionSpec as P

highest = lax.Precision.HIGHEST


def channel_grid(count):
    return (2.0 * jnp.arange(count, dtype=jnp.float32) - (count - 1)) / (count - 1)


def poly_gains(coefs, points):
    total = jnp.zeros((points.shape[0],) + coefs.shape[1:], jnp.float32)
    for order in range(coefs.shape[0]):
        total = total + (points**order)[:, None, None, None] * coefs[order][None]
    return total


def project_poly(values, points, orders):
    return jnp.stack(
        [
            jnp.einsum("f,frdn->rdn", points**order, values, precision=highest)
            for order in range(orders)
        ]
    )


def make_onehot(direction, count):
    return (direction[:, None] == jnp.arange(count, dtype=jnp.int32)[None, :]).astype(jnp.float32)


def phase_tables(uvw_cols, comp_lm, factor):
    sky_east = comp_lm[0]
    sky_north = comp_lm[1]
    sky_depth = jnp.sqrt(1.0 - sky_east * sky_east - sky_north * sky_north) - 1.0
    projected = (
        uvw_cols[0][:, None] * sky_east[None, :]
        + uvw_cols[1][:, None] * sky_north[None, :]
        + uvw_cols[2][:, None] * sky_depth[None, :]
    )
    angle = 2.0 * math.pi * factor * projected
    return (jnp.cos(angle), jnp.sin(angle))


def dot_rows(left, right):
    return lax.dot_general(
        left, right, (((1,), (1,)), ((), ())), preferred_element_type=jnp.float32
    )


def dot_cols(left, right):
    return lax.dot_general(
        left, right, (((0,), (0,)), ((), ())), preferred_element_type=jnp.float32
    )


def block_pass(
    vis_pair, weight, row_uvw, col_uvw, row_gain, col_gain, comp_lm, intensity, onehot, point
):
    factor = 1.0 + 0.15 * point
    row_cos, row_sin = phase_tables(row_uvw, comp_lm, factor)
    col_cos, col_sin = phase_tables(col_uvw, comp_lm, factor)
    left_real = ((row_gain[0] * row_cos + row_gain[1] * row_sin) * intensity).astype(jnp.bfloat16)
    left_imag = ((row_gain[1] * row_cos - row_gain[0] * row_sin) * intensity).astype(jnp.bfloat16)
    right_real = (col_gain[0] * col_cos + col_gain[1] * col_sin).astype(jnp.bfloat16)
    right_imag = (col_gain[1] * col_cos - col_gain[0] * col_sin).astype(jnp.bfloat16)
    left_both = jnp.concatenate([left_real, left_imag], axis=1)
    model_real = dot_rows(left_both, jnp.concatenate([right_real, right_imag], axis=1))
    model_imag = dot_rows(left_both, jnp.concatenate([-right_imag, right_real], axis=1))
    width = vis_pair.shape[1] // 2
    resid_real = (weight * (vis_pair[:, :width].astype(jnp.float32) - model_real)).astype(
        jnp.bfloat16
    )
    resid_imag = (weight * (vis_pair[:, width:].astype(jnp.float32) - model_imag)).astype(
        jnp.bfloat16
    )
    toward_real = jnp.dot(resid_real, right_real, preferred_element_type=jnp.float32) - jnp.dot(
        resid_imag, right_imag, preferred_element_type=jnp.float32
    )
    toward_imag = jnp.dot(resid_real, right_imag, preferred_element_type=jnp.float32) + jnp.dot(
        resid_imag, right_real, preferred_element_type=jnp.float32
    )
    row_real = intensity * (row_cos * toward_real - row_sin * toward_imag)
    row_imag = intensity * (row_cos * toward_imag + row_sin * toward_real)
    back_real = dot_cols(resid_real, left_real) + dot_cols(resid_imag, left_imag)
    back_imag = dot_cols(resid_real, left_imag) - dot_cols(resid_imag, left_real)
    col_real = col_cos * back_real - col_sin * back_imag
    col_imag = col_cos * back_imag + col_sin * back_real
    row_terms = -jnp.stack(
        [jnp.dot(row_real, onehot, precision=highest), jnp.dot(row_imag, onehot, precision=highest)]
    )
    col_terms = -jnp.stack(
        [jnp.dot(col_real, onehot, precision=highest), jnp.dot(col_imag, onehot, precision=highest)]
    )
    return (row_terms, col_terms)


def task_terms(vis_task, entry, flag_all, station_uvw, comp_lm, intensity, onehot, gains, points):
    block = vis_task.shape[2]
    half = vis_task.shape[0]
    row_start = entry[0] * block
    col_start = entry[1] * block
    kind = entry[2]
    row_gains = jnp.einsum(
        "crds,kd->crsk",
        lax.dynamic_slice_in_dim(gains, row_start, block, 3),
        onehot,
        precision=highest,
    )
    col_gains = jnp.einsum(
        "crds,kd->crsk",
        lax.dynamic_slice_in_dim(gains, col_start, block, 3),
        onehot,
        precision=highest,
    )
    row_flags = lax.dynamic_slice_in_dim(flag_all, row_start, block, 1)
    col_flags = lax.dynamic_slice_in_dim(flag_all, col_start, block, 1)
    row_uvw = lax.dynamic_slice_in_dim(station_uvw, row_start, block, 2)
    col_uvw = lax.dynamic_slice_in_dim(station_uvw, col_start, block, 2)
    across = jnp.arange(block, dtype=jnp.int32)
    upper = (across[:, None] < across[None, :]).astype(jnp.float32)
    lower = (across[:, None] > across[None, :]).astype(jnp.float32)
    first_mask = jnp.where(kind == 2, upper, jnp.ones_like(upper))
    channel_pass = jax.vmap(block_pass, in_axes=(0, None, None, None, 0, 0, None, None, None, 0))

    def pass_at(vis_time, moment, mask):
        weight = row_flags[moment][:, None] * col_flags[moment][None, :] * mask
        return channel_pass(
            vis_time,
            weight,
            row_uvw[moment],
            col_uvw[moment],
            row_gains,
            col_gains,
            comp_lm,
            intensity,
            onehot,
            points,
        )

    def one_time(carry, item):
        vis_time, moment = item
        first_row, first_col = pass_at(
            vis_time, moment + half * (kind == 1).astype(jnp.int32), first_mask
        )

        def with_second(unused):
            second_row, second_col = pass_at(vis_time, moment + half, lower)
            return (first_row + second_row, first_col + second_col)

        def alone(unused):
            return (first_row, first_col)

        row_terms, col_terms = lax.cond(kind == 2, with_second, alone, 0)
        return ((carry[0] + row_terms, carry[1] + col_terms), None)

    zeros = jnp.zeros((points.shape[0], 2, block, onehot.shape[1]), jnp.float32)
    sums, unused = lax.scan(one_time, (zeros, zeros), (vis_task, jnp.arange(half, dtype=jnp.int32)))
    return (jnp.swapaxes(sums[0], 2, 3), jnp.swapaxes(sums[1], 2, 3), row_start, col_start)


def add_block(total, piece, start):
    last = total.ndim - 1
    current = lax.dynamic_slice_in_dim(total, start, piece.shape[last], last)
    return lax.dynamic_update_slice_in_dim(total, current + piece, start, last)


def on_device(visibility, tasks, flags, station_uvw, comp_lm, intensity, direction, coefs):
    local_count = visibility.shape[2]
    channels = local_count * lax.axis_size("freq")
    points_all = channel_grid(channels)
    offset = lax.axis_index("freq") * local_count
    points = lax.dynamic_slice_in_dim(points_all, offset, local_count, 0)
    directions = coefs.shape[2]
    orders = coefs.shape[0]
    onehot = make_onehot(direction, directions)
    coef_all, flag_all = (
        lax.all_gather(coefs, ("row", "col"), axis=3, tiled=True),
        lax.all_gather(flags.astype(jnp.float32), ("row", "col"), axis=1, tiled=True),
    )
    gains = poly_gains(coef_all, points)
    row_part, col_part, row_start, col_start = task_terms(
        visibility[0], tasks[0], flag_all, station_uvw, comp_lm, intensity, onehot, gains, points
    )
    stations = flag_all.shape[1]
    spread = jnp.zeros((orders, 2, directions, stations), jnp.float32)
    spread = add_block(spread, project_poly(row_part, points, orders), row_start)
    spread = add_block(spread, project_poly(col_part, points, orders), col_start)
    owned = lax.psum_scatter(spread, ("row", "col"), scatter_dimension=3, tiled=True)
    summed = lax.psum(owned, "freq")
    return summed * (1.0 / math.sqrt(station_uvw.shape[0] * channels * stations))


def solution(mesh):
    return jax.shard_map(
        on_device,
        mesh=mesh,
        in_specs=(
            P(("row", "col"), None, "freq", None, None),
            P(("row", "col"), None),
            P(None, ("row", "col")),
            P(),
            P(),
            P(),
            P(),
            P(None, None, None, ("row", "col")),
        ),
        out_specs=P(None, None, None, ("row", "col")),
        check_vma=False,
    )
```

profile of v0, /device:TPU:0, one launch (start us, length us, event | category | flops | bytes accessed | tf_op | source)
XLA Modules:
  0.0 926.6 jit_solution(7153751037835235245)
XLA Ops:
  10.1 53.0 %all_gather.7 = f32[4,2,8,256]{2,0,1,3:T(4,128)S(1)} all-gather(f32[4,2,8,16]{2,0,1,3:T(4,128)S(1)} %copy.31), channel_id=1, replica_groups=mesh['row'=4,'col'=4,'freq'=2] {'row','col'}, dimensions={3}, use_global_device_ids=true | all-gather | bytes 69632 | tf_op jit(solution)/shard_map/all_gather | solution.py:181
  68.1 36.5 %all_gather.6 = f32[16,256]{0,1:T(8,128)S(1)} all-gather(f32[16,16]{0,1:T(8,128)S(1)} %convert_element_type.91), channel_id=1, replica_groups=mesh['row'=4,'col'=4,'freq'=2] {'row','col'}, dimensions={1}, use_global_device_ids=true | all-gather | bytes 17408 | tf_op jit(solution)/shard_map/all_gather | solution.py:182
  106.1 417.3 %while.17 = (s32[]{:T(128)}, f32[8,2,64,8]{2,3,0,1:T(8,128)S(1)}, f32[8,2,64,8]{2,3,0,1:T(8,128)S(1)}, pred[]{:T(512)}, f32[512]{0:T(512)S(1)}, /*index=5*/f32[8...) while((s32[]{:T(128)}, f32[8,2,64,8]{2,3,0,1:T(8,128)S(1)}, ...), condition=%wide.region_3.4_spmd.clone.clone.clone, body=%wide.region_0.3_spmd.clone.clone.clone.sunk | while | flops 1048903744 | bytes 81687536 | solution.py:161
  107.8 9.5 %fusion.313 = (bf16[8,64,512]{2,1,0:T(8,128)(2,1)S(1)}, bf16[8,64,512]{2,1,0:T(8,128)(2,1)S(1)}, bf16[8,64,512]{2,1,0:T(8,128)(2,1)S(1)}) fusion(f32[8,2,64,512]{3,2,0,1:T(8,128)} %get-tuple-element.808, f32[64,512]{1,0:T(8,128)S(1)} %get-tuple-element.736, f32[8]{0:T(128)S(1)} %add_multiply_fusion.4, f32[512]{0:T(512)S(1)} %get-tuple-element.797, ...), kind=kLoop, calls=%fused_computation.135.clone.1 | loop fusion | flops 4194304 | bytes 6031392 | tf_op jit(solution)/shard_map/while/body/eval_jaxpr/vmap()/convert_element_type | solution.py:66
  136.2 5.7 convolution_bitcast_fusion.13
  141.9 5.2 convolution_bitcast_fusion.12
  159.8 9.5 %fusion.313 = (bf16[8,64,512]{2,1,0:T(8,128)(2,1)S(1)}, bf16[8,64,512]{2,1,0:T(8,128)(2,1)S(1)}, bf16[8,64,512]{2,1,0:T(8,128)(2,1)S(1)}) fusion(f32[8,2,64,512]{3,2,0,1:T(8,128)} %get-tuple-element.808, f32[64,512]{1,0:T(8,128)S(1)} %get-tuple-element.736, f32[8]{0:T(128)S(1)} %add_multiply_fusion.4, f32[512]{0:T(512)S(1)} %get-tuple-element.797, ...), kind=kLoop, calls=%fused_computation.135.clone.1 | loop fusion | flops 4194304 | bytes 6031392 | tf_op jit(solution)/shard_map/while/body/eval_jaxpr/vmap()/convert_element_type | solution.py:66
  188.3 5.3 convolution_bitcast_fusion.13
  193.6 5.2 convolution_bitcast_fusion.12
  211.5 9.5 %fusion.313 = (bf16[8,64,512]{2,1,0:T(8,128)(2,1)S(1)}, bf16[8,64,512]{2,1,0:T(8,128)(2,1)S(1)}, bf16[8,64,512]{2,1,0:T(8,128)(2,1)S(1)}) fusion(f32[8,2,64,512]{3,2,0,1:T(8,128)} %get-tuple-element.808, f32[64,512]{1,0:T(8,128)S(1)} %get-tuple-element.736, f32[8]{0:T(128)S(1)} %add_multiply_fusion.4, f32[512]{0:T(512)S(1)} %get-tuple-element.797, ...), kind=kLoop, calls=%fused_computation.135.clone.1 | loop fusion | flops 4194304 | bytes 6031392 | tf_op jit(solution)/shard_map/while/body/eval_jaxpr/vmap()/convert_element_type | solution.py:66
  239.9 5.6 convolution_bitcast_fusion.13
  245.5 5.2 convolution_bitcast_fusion.12
  263.4 9.5 %fusion.313 = (bf16[8,64,512]{2,1,0:T(8,128)(2,1)S(1)}, bf16[8,64,512]{2,1,0:T(8,128)(2,1)S(1)}, bf16[8,64,512]{2,1,0:T(8,128)(2,1)S(1)}) fusion(f32[8,2,64,512]{3,2,0,1:T(8,128)} %get-tuple-element.808, f32[64,512]{1,0:T(8,128)S(1)} %get-tuple-element.736, f32[8]{0:T(128)S(1)} %add_multiply_fusion.4, f32[512]{0:T(512)S(1)} %get-tuple-element.797, ...), kind=kLoop, calls=%fused_computation.135.clone.1 | loop fusion | flops 4194304 | bytes 6031392 | tf_op jit(solution)/shard_map/while/body/eval_jaxpr/vmap()/convert_element_type | solution.py:66
  291.8 5.3 convolution_bitcast_fusion.13
  297.2 5.2 convolution_bitcast_fusion.12
  315.0 9.5 %fusion.313 = (bf16[8,64,512]{2,1,0:T(8,128)(2,1)S(1)}, bf16[8,64,512]{2,1,0:T(8,128)(2,1)S(1)}, bf16[8,64,512]{2,1,0:T(8,128)(2,1)S(1)}) fusion(f32[8,2,64,512]{3,2,0,1:T(8,128)} %get-tuple-element.808, f32[64,512]{1,0:T(8,128)S(1)} %get-tuple-element.736, f32[8]{0:T(128)S(1)} %add_multiply_fusion.4, f32[512]{0:T(512)S(1)} %get-tuple-element.797, ...), kind=kLoop, calls=%fused_computation.135.clone.1 | loop fusion | flops 4194304 | bytes 6031392 | tf_op jit(solution)/shard_map/while/body/eval_jaxpr/vmap()/convert_element_type | solution.py:66
  343.5 5.6 convolution_bitcast_fusion.13
  366.9 9.5 %fusion.313 = (bf16[8,64,512]{2,1,0:T(8,128)(2,1)S(1)}, bf16[8,64,512]{2,1,0:T(8,128)(2,1)S(1)}, bf16[8,64,512]{2,1,0:T(8,128)(2,1)S(1)}) fusion(f32[8,2,64,512]{3,2,0,1:T(8,128)} %get-tuple-element.808, f32[64,512]{1,0:T(8,128)S(1)} %get-tuple-element.736, f32[8]{0:T(128)S(1)} %add_multiply_fusion.4, f32[512]{0:T(512)S(1)} %get-tuple-element.797, ...), kind=kLoop, calls=%fused_computation.135.clone.1 | loop fusion | flops 4194304 | bytes 6031392 | tf_op jit(solution)/shard_map/while/body/eval_jaxpr/vmap()/convert_element_type | solution.py:66
  395.4 5.3 convolution_bitcast_fusion.13
  418.6 9.5 %fusion.313 = (bf16[8,64,512]{2,1,0:T(8,128)(2,1)S(1)}, bf16[8,64,512]{2,1,0:T(8,128)(2,1)S(1)}, bf16[8,64,512]{2,1,0:T(8,128)(2,1)S(1)}) fusion(f32[8,2,64,512]{3,2,0,1:T(8,128)} %get-tuple-element.808, f32[64,512]{1,0:T(8,128)S(1)} %get-tuple-element.736, f32[8]{0:T(128)S(1)} %add_multiply_fusion.4, f32[512]{0:T(512)S(1)} %get-tuple-element.797, ...), kind=kLoop, calls=%fused_computation.135.clone.1 | loop fusion | flops 4194304 | bytes 6031392 | tf_op jit(solution)/shard_map/while/body/eval_jaxpr/vmap()/convert_element_type | solution.py:66
  447.0 5.6 convolution_bitcast_fusion.13
  470.5 9.5 %fusion.313 = (bf16[8,64,512]{2,1,0:T(8,128)(2,1)S(1)}, bf16[8,64,512]{2,1,0:T(8,128)(2,1)S(1)}, bf16[8,64,512]{2,1,0:T(8,128)(2,1)S(1)}) fusion(f32[8,2,64,512]{3,2,0,1:T(8,128)} %get-tuple-element.808, f32[64,512]{1,0:T(8,128)S(1)} %get-tuple-element.736, f32[8]{0:T(128)S(1)} %add_multiply_fusion.4, f32[512]{0:T(512)S(1)} %get-tuple-element.797, ...), kind=kLoop, calls=%fused_computation.135.clone.1 | loop fusion | flops 4194304 | bytes 6031392 | tf_op jit(solution)/shard_map/while/body/eval_jaxpr/vmap()/convert_element_type | solution.py:66
  498.9 5.3 convolution_bitcast_fusion.13
  530.5 384.1 %reduce-scatter.4.cloned.1.call-done = f32[16,64]{1,0:T(8,128)} async-done(((f32[256,64]{1,0:T(8,128)}), f32[16,64]{1,0:T(8,128)}) %reduce-scatter.4.cloned.1.call-update) | async-done | bytes 4112
  (317 shorter events, 206.8 us)
Async XLA Ops:
  6.5 908.0 %reduce-scatter.4.cloned.1.call-start = ((), (), s32[]{:S(2)}) async-start(), calls=%async_computation.1 | async-start | bytes 139264
  63.1 1.5 copy-start.1
  64.6 3.4 copy-start.4
  64.6 40.1 %copy-start.3 = (f32[16,3,256]{2,0,1:T(8,128)S(1)}, f32[16,3,256]{2,0,1:T(8,128)}, u32[]{:S(2)}) copy-start(f32[16,3,256]{2,0,1:T(8,128)} %param.15) | copy-start | bytes 147460
  64.6 41.5 %copy-start.2 = (f32[2,512]{1,0:T(2,128)S(1)}, f32[2,512]{1,0:T(2,128)}, u32[]{:S(2)}) copy-start(f32[2,512]{1,0:T(2,128)} %param.16) | copy-start | bytes 12292
  64.6 41.5 %copy-start = (f32[512]{0:T(512)S(1)}, f32[512]{0:T(512)}, u32[]{:S(2)}) copy-start(f32[512]{0:T(512)} %param.17) | copy-start | bytes 6148
Sparse Core Ops, SparseCore 0:
  530.6 383.8 reduce-scatter.3
where the time goes:
time: 931 us; the launch traced here: 927 us
  waiting for transfers between devices  384 us (41%)
  matrix products  199 us (21%)
  other arithmetic  113 us (12%)
  loops' own time  98.8 us (11%)
  blocking collectives  92.9 us (10%)
  local copies, waits for them, and re-layouts  22.5 us (2%)
  between operations  16.3 us (2%)
    unnamed x2, waiting for transfers between devices  384 us
    another operation x1, loops' own time, task_terms(): lax.scan(one_time, (zeros, zeros), (vis_task, jnp.arange(half, dtype=jnp....  89.6 us
    convert_element_type x8, other arithmetic, block_pass(): ((row_gain[0] * row_cos + row_gain[1] * row_sin) * intensity).astype(jnp....  75.8 us
    all_gather x1, blocking collectives, on_device(): lax.all_gather(coefs, ('row', 'col'), axis=3, tiled=True)  53 us
    dot_general x8, matrix products, block_pass(): jnp.dot(row_real, onehot, precision=highest)  43.8 us
    dot_general x8, matrix products, block_pass(): jnp.dot(row_imag, onehot, precision=highest)  41.5 us
    dot_general x8, matrix products, block_pass(): jnp.dot(col_imag, onehot, precision=highest)  41.3 us
    dot_general x8, matrix products, block_pass(): jnp.dot(col_real, onehot, precision=highest)  41.1 us
  transfers between devices with their start and end apart: 1, of which 1 were waited for; matrix products, arithmetic and copies ran while one was open for 0% of the time, Pallas kernels for 0%

commit v1 on v0

v1 whole, which is shorter than its diff:
```python
import functools
import math

import jax
import jax.numpy as jnp
import numpy as np
from jax import lax
from jax.experimental import pallas as pl
from jax.experimental.pallas import tpu as pltpu
from jax.sharding import PartitionSpec as P

MESH = pl.DeviceIdType.MESH
LANES = 128
F32 = jnp.float32


def fit_even(function, terms):
    nodes = 0.25 * (1.0 - np.cos(np.pi * (np.arange(400) + 0.5) / 400)) / 2.0
    values = function(np.sqrt(nodes))
    basis = np.stack([nodes**n for n in range(terms)], axis=1)
    return [float(c) for c in np.linalg.lstsq(basis, values, rcond=None)[0]]


SIN_FIT = fit_even(lambda r: np.sin(np.pi * r) / r, 5)
COS_FIT = fit_even(lambda r: np.cos(np.pi * r), 6)


def horner(coefficients, z):
    total = jnp.full_like(z, coefficients[-1])
    for c in coefficients[-2::-1]:
        total = total * z + c
    return total


def turn_cos_sin(turns):
    r = turns - jnp.round(turns)
    z = r * r
    s = horner(SIN_FIT, z) * r
    c = horner(COS_FIT, z)
    return 1.0 - 2.0 * (s * s), 2.0 * (s * c)


def others(sizes, axes, body):
    count = math.prod(sizes)
    me = 0
    for size, axis in zip(sizes, axes):
        me = me * size + lax.axis_index(axis)

    def step(j, unused):
        rest = lax.rem(me + j + 1, count)
        where = {}
        for size, axis in zip(sizes[::-1], axes[::-1]):
            where[axis] = lax.rem(rest, size)
            rest = rest // size
        body(j, where)
        return unused

    lax.fori_loop(0, count - 1, step, 0)
    return me


def greet(sizes, axes):
    barrier = pltpu.get_barrier_semaphore()

    def signal(j, where):
        pl.semaphore_signal(barrier, inc=1, device_id=where, device_id_type=MESH)

    me = others(sizes, axes, signal)
    pl.semaphore_wait(barrier, math.prod(sizes) - 1)
    return me


def put_lanes(piece, start):
    rows, width = piece.shape
    parts = []
    if start:
        parts.append(jnp.zeros((rows, start), piece.dtype))
    parts.append(piece)
    if start + width < LANES:
        parts.append(jnp.zeros((rows, LANES - start - width), piece.dtype))
    return jnp.concatenate(parts, axis=1) if len(parts) > 1 else piece


def gather_kernel(sizes, coef_ref, flag_ref, all_ref, mine, send_sem, recv_sem, own_sem):
    axes = ("row", "col")
    width = coef_ref.shape[1]
    for base, ref in ((0, coef_ref), (8, flag_ref)):
        tile = jnp.zeros((8, LANES), F32)
        for g in range(ref.shape[0] // 8):
            tile = tile + put_lanes(ref[8 * g : 8 * g + 8, :].astype(F32), g * width)
        mine[base : base + 8, :] = tile
    me = greet(sizes, axes)

    def send(j, where):
        pltpu.make_async_remote_copy(
            src_ref=mine,
            dst_ref=all_ref.at[me],
            send_sem=send_sem,
            recv_sem=recv_sem,
            device_id=where,
            device_id_type=MESH,
        ).start()

    others(sizes, axes, send)
    own = pltpu.make_async_copy(mine, all_ref.at[me], own_sem)
    own.start()
    own.wait()
    rest = all_ref.at[pl.ds(0, math.prod(sizes) - 1)]
    done = pltpu.make_async_remote_copy(
        src_ref=rest,
        dst_ref=rest,
        send_sem=send_sem,
        recv_sem=recv_sem,
        device_id={axis: lax.axis_index(axis) for axis in axes},
        device_id_type=MESH,
    )
    done.wait_send()
    done.wait_recv()


def reduce_kernel(sizes, part_ref, out_ref, held, send_sem, recv_sem):
    axes = ("row", "col", "freq")
    me = greet(sizes, axes)
    groups = sizes[2]

    def send(j, where):
        owner = where["row"] * sizes[1] + where["col"]
        pltpu.make_async_remote_copy(
            src_ref=part_ref.at[owner],
            dst_ref=held.at[j],
            send_sem=send_sem,
            recv_sem=recv_sem,
            device_id=where,
            device_id_type=MESH,
        ).start()

    others(sizes, axes, send)
    done = pltpu.make_async_remote_copy(
        src_ref=held,
        dst_ref=held,
        send_sem=send_sem,
        recv_sem=recv_sem,
        device_id={axis: lax.axis_index(axis) for axis in axes},
        device_id_type=MESH,
    )
    done.wait_send()
    done.wait_recv()
    total = part_ref[me // groups] + jnp.sum(held[...], axis=0)
    width = out_ref.shape[1]
    for g in range(out_ref.shape[0] // 8):
        out_ref[8 * g : 8 * g + 8, :] = total[:, g * width : (g + 1) * width]


def halves_swapped(x):
    return jnp.concatenate([x[:, LANES // 2 :], x[:, : LANES // 2]], axis=1)


def work_kernel(
    width,
    channels,
    task_ref,
    point_ref,
    all_ref,
    vis_ref,
    uvw_ref,
    lm_ref,
    intensity_ref,
    direction_ref,
    out_ref,
    gains,
    flags,
    sky,
    weight,
    step_table,
    phase,
    x_ref,
    sums,
):
    times, local, block = vis_ref.shape[0], vis_ref.shape[1], vis_ref.shape[2]
    comps = sky.shape[1]
    directions = gains.shape[2]
    each = comps // directions
    orders = 4
    owners = block // width
    first, second, kind = task_ref[0, 0], task_ref[0, 1], task_ref[0, 2]
    paired = kind == 2
    lane = lax.broadcasted_iota(jnp.int32, (8, LANES), 1)
    on_a = lane < block

    for g in range(2 * orders + flags.shape[0] // 8):
        base, at = (0, g) if g < 2 * orders else (8, g - 2 * orders)
        tile = jnp.zeros((8, LANES), F32)
        for side, blk in ((0, first), (1, second)):
            for i in range(owners):
                piece = all_ref[blk * owners + i, base : base + 8, at * width : (at + 1) * width]
                tile = tile + put_lanes(piece, side * block + i * width)
        if g < 2 * orders:
            sums[0, 0, g] = tile
        else:
            flags[8 * at : 8 * at + 8, :] = tile
    for f in range(local):
        x = point_ref[0, f]
        for c in range(2):
            value = sums[0, 0, 2 * orders - 2 + c]
            for n in range(orders - 2, -1, -1):
                value = value * x + sums[0, 0, 2 * n + c]
            gains[f, c] = value

    drow = direction_ref[...].astype(F32)
    count = jnp.zeros((1, comps), F32)
    krow = lax.broadcasted_iota(jnp.int32, (LANES, comps), 1)
    jcol = lax.broadcasted_iota(jnp.int32, (LANES, comps), 0)
    for j in range(comps // LANES):
        piece = jnp.broadcast_to(drow[:, j * LANES : (j + 1) * LANES], (LANES, LANES))
        column = jnp.transpose(piece)
        column = jnp.concatenate([column] * (comps // LANES), axis=1)
        same = jnp.logical_and(column == drow, jcol + j * LANES < krow)
        count = count + jnp.sum(same.astype(F32), axis=0, keepdims=True)
    place = (drow * each + count).astype(jnp.int32)
    east, north = lm_ref[0:1, :], lm_ref[1:2, :]
    depth = jnp.sqrt(1.0 - east * east - north * north) - 1.0
    bright = intensity_ref[...]
    for d in range(directions):
        rows = pl.ds(d * each, each)
        here = lax.broadcasted_iota(jnp.int32, (each, comps), 0) + d * each == place
        for n, value in enumerate((east, north, depth, bright)):
            column = jnp.sum(jnp.where(here, value, 0.0), axis=1, keepdims=True)
            if n < 3:
                sky[n, rows, :] = jnp.broadcast_to(column, (each, LANES))
            else:
                wide = jnp.broadcast_to(column, (each, LANES))
                mixed = lax.broadcasted_iota(jnp.int32, (each, LANES), 1) < block
                sky[3, rows, :] = jnp.where(paired, jnp.sqrt(wide), jnp.where(mixed, wide, 1.0))

    i = lax.broadcasted_iota(jnp.int32, (block, LANES), 0)
    j = lax.broadcasted_iota(jnp.int32, (block, LANES), 1)
    left = j < block
    j = jnp.where(left, j, j - block)
    one, zero = jnp.float32(1.0), jnp.float32(0.0)
    upper = (i < j).astype(F32)
    lower = (i > j).astype(F32)
    leftf = left.astype(F32)
    pick_a = jnp.where(paired, upper, one)
    pick_b = jnp.where(paired, lower, zero)
    unequal = upper + lower
    mask_a = jnp.where(paired, unequal * leftf, 1.0 - leftf)
    mask_b = jnp.where(paired, unequal * (1.0 - leftf), leftf)

    sums[...] = jnp.zeros_like(sums)
    late_a = jnp.where(kind == 1, times, 0)
    late_b = jnp.where(kind == 0, 0, times)
    factor = 1.0 + 0.15 * point_ref[0, 0]
    spacing = 0.15 * 2.0 / (channels - 1)

    def side_tile(ref, blk, side, moment):
        tile = ref[moment, :, pl.ds(pl.multiple_of((blk // 2) * LANES, LANES), LANES)]
        return jnp.where(lax.rem(blk, 2) == side, tile, halves_swapped(tile))

    def make_x(f, slot):
        for d in range(directions):
            rows = pl.ds(d * each, each)
            if f == 0:
                c, s = phase[0, 0, rows, :], phase[0, 1, rows, :]
            else:
                c0, s0 = phase[1 - slot, 0, rows, :], phase[1 - slot, 1, rows, :]
                ec, es = step_table[0, rows, :], step_table[1, rows, :]
                c = c0 * ec - s0 * es
                s = s0 * ec + c0 * es
                phase[slot, 0, rows, :] = c
                phase[slot, 1, rows, :] = s
            gr, gi = gains[f, 0, d : d + 1, :], gains[f, 1, d : d + 1, :]
            x_ref[slot, rows, 0:LANES] = (gr * c + gi * s).astype(jnp.bfloat16)
            x_ref[slot, rows, LANES : 2 * LANES] = (gi * c - gr * s).astype(jnp.bfloat16)

    def one_time(t, unused):
        tau_a, tau_b = t + late_a, t + late_b
        uvw = jnp.where(
            lax.broadcasted_iota(jnp.int32, (3, LANES), 1) < block,
            side_tile(uvw_ref, first, 0, tau_a),
            side_tile(uvw_ref, second, 1, tau_b),
        )
        good = jnp.where(
            lax.broadcasted_iota(jnp.int32, (1, LANES), 1) < block,
            flags[pl.ds(tau_a, 1), :],
            flags[pl.ds(tau_b, 1), :],
        )
        good = jnp.broadcast_to(good, (LANES, LANES))
        both = good * jnp.transpose(good)
        weight[0:block, :] = both[0:block] * mask_a
        weight[block : 2 * block, :] = both[block : 2 * block] * mask_b
        for d in range(directions):
            rows = pl.ds(d * each, each)
            turns = (
                sky[0, rows, :] * uvw[0:1] + sky[1, rows, :] * uvw[1:2] + sky[2, rows, :] * uvw[2:3]
            )
            c, s = turn_cos_sin(turns * factor)
            phase[0, 0, rows, :] = c * sky[3, rows, :]
            phase[0, 1, rows, :] = s * sky[3, rows, :]
            c, s = turn_cos_sin(turns * spacing)
            step_table[0, rows, :] = c
            step_table[1, rows, :] = s
        make_x(0, 0)
        for f in range(local):
            slot = f % 2
            x = x_ref[slot]
            z = lax.dot_general(x, x, (((0,), (0,)), ((), ())), preferred_element_type=F32)
            if f + 1 < local:
                make_x(f + 1, 1 - slot)
            v = vis_ref[t, f].astype(F32)
            turned = jnp.transpose(jnp.concatenate([v, v], axis=0))
            swapped = halves_swapped(v)
            real, imag = jnp.where(left, v, swapped), jnp.where(left, swapped, v)
            model_r = z[0:LANES, 0:LANES] + z[LANES:, LANES:]
            model_i = z[0:LANES, LANES:] - z[LANES:, 0:LANES]
            parts_r, parts_i = [], []
            for side, pick in ((0, pick_a), (1, pick_b)):
                rows = slice(side * block, (side + 1) * block)
                want = pick > 0.5
                vr = jnp.where(want, real, turned[0:block])
                vi = jnp.where(want, -imag, turned[block:])
                w = weight[rows, :]
                parts_r.append(w * (vr - model_r[rows]))
                parts_i.append(w * (vi - model_i[rows]))
            er = jnp.concatenate(parts_r, axis=0).astype(jnp.bfloat16)
            ei = jnp.concatenate(parts_i, axis=0).astype(jnp.bfloat16)
            e = jnp.concatenate(
                [jnp.concatenate([er, ei], axis=1), jnp.concatenate([-ei, er], axis=1)], axis=0
            )
            h = jnp.dot(x, e, preferred_element_type=F32)
            for d in range(directions):
                rows = slice(d * each, (d + 1) * each)
                c, s = phase[slot, 0, rows, :], phase[slot, 1, rows, :]
                hr, hi = h[rows, 0:LANES], h[rows, LANES:]
                tr = jnp.sum((c * hr - s * hi).reshape(each // 8, 8, LANES), axis=0)
                ti = jnp.sum((c * hi + s * hr).reshape(each // 8, 8, LANES), axis=0)
                sums[f, 0, d] += tr
                sums[f, 1, d] += ti
        return unused

    lax.fori_loop(0, times, one_time, 0)

    scale = -1.0 / math.sqrt(2 * times * channels * out_ref.shape[0] * width)
    out_ref[...] = jnp.zeros_like(out_ref)
    tiles = [None] * (2 * orders)
    for f in range(local):
        x = point_ref[0, f]
        for c in range(2):
            total = jnp.sum(sums[f, c], axis=1) * scale
            for n in range(orders):
                old = tiles[2 * n + c]
                tiles[2 * n + c] = total if old is None else old + total
                total = total * x
    for side, blk in ((0, first), (1, second)):
        for i in range(owners):
            start = side * block + i * width
            packed = [tiles[g][:, start : start + width] for g in range(2 * orders)]
            tile = jnp.concatenate(packed, axis=1)
            out_ref[blk * owners + i] += put_lanes(tile, 0)


def vmem():
    return pl.BlockSpec(memory_space=pltpu.VMEM)


def smem():
    return pl.BlockSpec(memory_space=pltpu.SMEM)


def on_device(sizes, visibility, tasks, flags, station_uvw, comp_lm, intensity, direction, coefs):
    rows, cols, parts = sizes
    devices = rows * cols
    orders, unused, directions, width = coefs.shape
    unused, times, local, block, unused = visibility.shape
    comps = direction.shape[0]
    channels = local * parts
    offset = lax.axis_index("freq") * local
    points = (
        2.0 * (offset + jnp.arange(local, dtype=jnp.int32)).astype(F32) - (channels - 1)
    ) / (channels - 1)

    gathered = pl.pallas_call(
        functools.partial(gather_kernel, (rows, cols)),
        out_shape=jax.ShapeDtypeStruct((devices, 16, LANES), F32),
        in_specs=[vmem()] * 2,
        out_specs=vmem(),
        scratch_shapes=[
            pltpu.VMEM((16, LANES), F32),
            pltpu.SemaphoreType.DMA,
            pltpu.SemaphoreType.DMA,
            pltpu.SemaphoreType.DMA,
        ],
        compiler_params=pltpu.CompilerParams(collective_id=0, has_side_effects=True),
        name="gather_gains",
    )(coefs.reshape(orders * 2 * directions, width), flags)

    terms = pl.pallas_call(
        functools.partial(work_kernel, width, channels),
        out_shape=jax.ShapeDtypeStruct((devices, directions, LANES), F32),
        in_specs=[smem(), smem()] + [vmem()] * 6,
        out_specs=vmem(),
        scratch_shapes=[
            pltpu.VMEM((local, 2, directions, LANES), F32),
            pltpu.VMEM((flags.shape[0], LANES), F32),
            pltpu.VMEM((4, comps, LANES), F32),
            pltpu.VMEM((LANES, LANES), F32),
            pltpu.VMEM((2, comps, LANES), F32),
            pltpu.VMEM((2, 2, comps, LANES), F32),
            pltpu.VMEM((2, comps, 2 * LANES), jnp.bfloat16),
            pltpu.VMEM((local, 2, directions, 8, LANES), F32),
        ],
        compiler_params=pltpu.CompilerParams(vmem_limit_bytes=48 * 1024 * 1024),
        name="gain_terms",
    )(
        tasks,
        points.reshape(1, local),
        gathered,
        visibility[0],
        station_uvw,
        comp_lm,
        intensity.reshape(1, comps),
        direction.reshape(1, comps),
    )

    out = pl.pallas_call(
        functools.partial(reduce_kernel, sizes),
        out_shape=jax.ShapeDtypeStruct((orders * 2 * directions, width), F32),
        in_specs=[vmem()],
        out_specs=vmem(),
        scratch_shapes=[
            pltpu.VMEM((devices * parts - 1, directions, LANES), F32),
            pltpu.SemaphoreType.DMA,
            pltpu.SemaphoreType.DMA,
        ],
        compiler_params=pltpu.CompilerParams(collective_id=1, has_side_effects=True),
        name="reduce_terms",
    )(terms)
    return out.reshape(orders, 2, directions, width)


def solution(mesh):
    sizes = tuple(mesh.shape[axis] for axis in ("row", "col", "freq"))
    return jax.shard_map(
        functools.partial(on_device, sizes),
        mesh=mesh,
        in_specs=(
            P(("row", "col"), None, "freq", None, None),
            P(("row", "col"), None),
            P(None, ("row", "col")),
            P(),
            P(),
            P(),
            P(),
            P(None, None, None, ("row", "col")),
        ),
        out_specs=P(None, None, None, ("row", "col")),
        check_vma=False,
    )
```

time: 931 us -> 54.7 us (0.06)
  waiting for transfers between devices: 384 us -> 0 us
  matrix products: 199 us -> 0 us
  other arithmetic: 113 us -> 0.01 us
  loops' own time: 98.8 us -> 0 us
  blocking collectives: 92.9 us -> 0 us
  Pallas kernels: 0 us -> 49.2 us
  local copies, waits for them, and re-layouts: 22.5 us -> 4.98 us
  between operations: 16.3 us -> 0.11 us
    unnamed x2 -> x0, waiting for transfers between devices: 384 us -> none
    dot_general x122 -> x0, matrix products: 199 us -> none  [the longest x8 43.8 us: block_pass(): jnp.dot(row_real, onehot, precision=highest)]
    another operation x9 -> x0, loops' own time: 98.8 us -> none  [the longest x1 89.6 us: task_terms(): lax.scan(one_time, (zeros, zeros), (vis_task, jnp.arange(half, dtype=jnp....]
    all_gather x2 -> x0, blocking collectives: 89.5 us -> none  [the longest x1 53 us: on_device(): lax.all_gather(coefs, ('row', 'col'), axis=3, tiled=True)]
    convert_element_type x25 -> x0, other arithmetic: 75.9 us -> none  [the longest x8 75.8 us: block_pass(): ((row_gain[0] * row_cos + row_gain[1] * row_sin) * intensity).astype(jnp....]
    pallas_call x0 -> x3, Pallas kernels: none -> 49.2 us  [the longest x1 26.7 us: on_device(): pl.pallas_call(functools.partial(work_kernel, width, channels), out_shape...]
    neg x8 -> x0, other arithmetic: 33.6 us -> none  [block_pass(): -right_imag]
  transfers between devices with their start and end apart: 1 -> 0, of which waited for: 1 -> 0; matrix products, arithmetic and copies ran while one was open for 0% -> 0% of each run, Pallas kernels for 0% -> 0%
where the time goes in v1:
time: 54.7 us; the launch traced here: 54.3 us
  Pallas kernels  49.2 us (90%)
  local copies, waits for them, and re-layouts  4.98 us (9%)
    pallas_call x1, Pallas kernels, on_device(): pl.pallas_call(functools.partial(work_kernel, width, channels), out_shape...  26.7 us
    pallas_call x1, Pallas kernels, on_device(): pl.pallas_call(functools.partial(gather_kernel, (rows, cols)), out_shape=...  12.2 us
    pallas_call x1, Pallas kernels, on_device(): pl.pallas_call(functools.partial(reduce_kernel, sizes), out_shape=jax.Sha...  10.3 us
    unnamed x16, local copies, waits for them, and re-layouts  4.98 us

profile of v1, /device:TPU:0, one launch (start us, length us, event | category | flops | bytes accessed | tf_op | source)
XLA Modules:
  0.0 54.3 jit_solution(11178155240280203258)
XLA Ops:
  0.0 0.8 %copy.9.uvw_ref = f32[16,3,256]{2,1,0:T(4,128)S(1)} copy(f32[16,3,256]{2,0,1:T(8,128)} %param.11) | data formatting | bytes 98304 | tf_op args[3]
  0.8 0.0 copy-start.3
  0.9 0.0 copy-start.4
  0.9 0.0 copy-start.5
  0.9 0.0 copy-start.6
  0.9 12.2 %gather_gains.1.all_ref = f32[16,16,128]{2,1,0:T(8,128)} custom-call(f32[64,16]{1,0:T(8,128)} %bitcast.9, s32[16,16]{1,0:T(8,128)} %flag_ref.1), custom_call_target="tpu_custom_call" | custom-call | tf_op jit(solution)/shard_map/gather_gains/pallas_call | solution.py:381
  13.1 0.0 copy-done.3
  13.1 0.0 copy-done.4
  13.1 0.0 copy-done.5
  13.1 0.0 copy-done.6
  13.1 0.0 copy-start
  13.1 1.2 %copy-done = bf16[1,8,8,64,128]{4,3,2,1,0:T(8,128)(2,1)S(1)} copy-done((bf16[1,8,8,64,128]{4,3,2,1,0:T(8,128)(2,1)S(1)}, bf16[1,8,8,64,128]{4,3,2,1,0:T(8,128)(2,1)}, u32[]{:S(2)}) %copy-start) | copy-done | bytes 1048600
  14.4 0.0 copy-start.1
  14.4 0.9 %copy-done.1 = f32[16,16,128]{2,1,0:T(8,128)S(1)} copy-done((f32[16,16,128]{2,1,0:T(8,128)S(1)}, f32[16,16,128]{2,1,0:T(8,128)}, u32[]{:S(2)}) %copy-start.1) | copy-done | bytes 131096
  15.3 26.7 %gain_terms.1.part_ref = f32[16,8,128]{2,1,0:T(8,128)S(1)} custom-call(s32[1,3]{1,0:T(1,128)S(1)} %copy-done.6, f32[1,8]{1,0:T(1,128)S(1)} %add_multiply_fusion.point_ref, f32[16,16,128]{2,1,0:T(8,128)S(1)} %copy-done.1, bf16[8,8,64,128]{3,2,1,0:T(8,128)(2,1)S(1)} %bitcast.5, f32[16,3,256]{2,1,0:T(4,128)S(1)} %copy.9.uvw_ref, f32[2,512]{1,0:T(2,128)S(1)} %copy-done.3, ...), custom_call_target="tpu_custom_call" | custom-call | tf_op jit(solution)/shard_map/gain_terms/pallas_call | solution.py:396
  42.0 0.0 copy-start.2
  42.0 0.6 %copy-done.2 = f32[16,8,128]{2,1,0:T(8,128)} copy-done((f32[16,8,128]{2,1,0:T(8,128)}, f32[16,8,128]{2,1,0:T(8,128)S(1)}, u32[]{:S(2)}) %copy-start.2) | copy-done | bytes 65560
  42.6 10.3 %reduce_terms.1 = f32[64,16]{1,0:T(8,128)} custom-call(f32[16,8,128]{2,1,0:T(8,128)} %copy-done.2), custom_call_target="tpu_custom_call" | custom-call | tf_op jit(solution)/shard_map/reduce_terms/pallas_call | solution.py:424
  52.9 1.4 %copy.11 = f32[4,2,8,16]{3,2,1,0:T(8,128)} copy(f32[4,2,8,16]{3,2,1,0:T(8,128)} %bitcast.8) | data formatting | bytes 8192
  (1 shorter events, 0.0 us)
Async XLA Ops:
  0.8 12.2 %copy-start.3 = (f32[2,512]{1,0:T(2,128)S(1)}, f32[2,512]{1,0:T(2,128)}, u32[]{:S(2)}) copy-start(f32[2,512]{1,0:T(2,128)} %lm_ref.1) | copy-start | bytes 12292
  0.9 12.2 %copy-start.4 = (f32[512]{0:T(512)S(1)}, f32[512]{0:T(512)}, u32[]{:S(2)}) copy-start(f32[512]{0:T(512)} %param.13) | copy-start | bytes 6148
  0.9 12.2 %copy-start.5 = (s32[512]{0:T(512)S(1)}, s32[512]{0:T(512)}, u32[]{:S(2)}) copy-start(s32[512]{0:T(512)} %param.14) | copy-start | bytes 6148
  0.9 12.2 %copy-start.6 = (s32[1,3]{1,0:T(1,128)S(1)}, s32[1,3]{1,0:T(1,128)}, u32[]{:S(2)}) copy-start(s32[1,3]{1,0:T(1,128)} %task_ref.1) | copy-start | bytes 40
  13.1 1.2 %copy-start = (bf16[1,8,8,64,128]{4,3,2,1,0:T(8,128)(2,1)S(1)}, bf16[1,8,8,64,128]{4,3,2,1,0:T(8,128)(2,1)}, u32[]{:S(2)}) copy-start(bf16[1,8,8,64,128]{4,3,2,1,0:T(8,128)(2,1)} %param.8) | copy-start | bytes 3145732
  14.4 0.9 %copy-start.1 = (f32[16,16,128]{2,1,0:T(8,128)S(1)}, f32[16,16,128]{2,1,0:T(8,128)}, u32[]{:S(2)}) copy-start(f32[16,16,128]{2,1,0:T(8,128)} %gather_gains.1.all_ref) | copy-start | bytes 393220
  42.0 0.6 %copy-start.2 = (f32[16,8,128]{2,1,0:T(8,128)}, f32[16,8,128]{2,1,0:T(8,128)S(1)}, u32[]{:S(2)}) copy-start(f32[16,8,128]{2,1,0:T(8,128)S(1)} %gain_terms.1.part_ref) | copy-start | bytes 196612

commit v2 on v1

v2 whole, which is shorter than its diff:
```python
import functools
import math

import jax
import jax.numpy as jnp
import numpy as np
from jax import lax
from jax.experimental import pallas as pl
from jax.experimental.pallas import tpu as pltpu
from jax.sharding import PartitionSpec as P

MESH = pl.DeviceIdType.MESH
LANES = 128
F32 = jnp.float32


def fit_even(function, terms):
    nodes = 0.25 * (1.0 - np.cos(np.pi * (np.arange(400) + 0.5) / 400)) / 2.0
    values = function(np.sqrt(nodes))
    basis = np.stack([nodes**n for n in range(terms)], axis=1)
    return [float(c) for c in np.linalg.lstsq(basis, values, rcond=None)[0]]


SIN_FIT = fit_even(lambda r: np.sin(np.pi * r) / r, 5)
COS_FIT = fit_even(lambda r: np.cos(np.pi * r), 6)


def horner(coefficients, z):
    total = jnp.full_like(z, coefficients[-1])
    for c in coefficients[-2::-1]:
        total = total * z + c
    return total


def turn_cos_sin(turns):
    r = turns - jnp.round(turns)
    z = r * r
    s = horner(SIN_FIT, z) * r
    c = horner(COS_FIT, z)
    return 1.0 - 2.0 * (s * s), 2.0 * (s * c)


def walk(sizes, axes, body):
    count = math.prod(sizes)
    moved = [
        [lax.rem(lax.axis_index(axis) + step, size) for step in range(size)] if count <= 64 else None
        for size, axis in zip(sizes, axes)
    ]

    def far(j, unused):
        rest, where = j + 1, {}
        for size, axis in zip(sizes[::-1], axes[::-1]):
            where[axis] = lax.rem(lax.axis_index(axis) + lax.rem(rest, size), size)
            rest = rest // size
        body(j, where)
        return unused

    if count > 64:
        lax.fori_loop(0, count - 1, far, 0)
        return
    for j in range(count - 1):
        rest, where = j + 1, {}
        for n in range(len(sizes) - 1, -1, -1):
            where[axes[n]] = moved[n][rest % sizes[n]]
            rest = rest // sizes[n]
        body(j, where)


def put_lanes(piece, start):
    rows, width = piece.shape
    parts = []
    if start:
        parts.append(jnp.zeros((rows, start), piece.dtype))
    parts.append(piece)
    if start + width < LANES:
        parts.append(jnp.zeros((rows, LANES - start - width), piece.dtype))
    return jnp.concatenate(parts, axis=1) if len(parts) > 1 else piece


def halves_swapped(x):
    half = x.shape[-1] // 2
    return jnp.concatenate([x[..., half:], x[..., :half]], axis=-1)


def kernel(
    sizes,
    task_ref,
    coef_ref,
    flag_ref,
    vis_hbm,
    uvw_ref,
    lm_ref,
    intensity_ref,
    direction_ref,
    out_ref,
    all_ref,
    part_ref,
    held,
    vis_ref,
    coef_tiles,
    gains,
    flags,
    places,
    sky,
    weight,
    step_table,
    phase,
    x_ref,
    z_ref,
    sums,
    gather_send,
    gather_recv,
    reduce_send,
    reduce_recv,
    vis_sem,
):
    times, local, block = vis_ref.shape[0], vis_ref.shape[1], vis_ref.shape[2]
    comps = sky.shape[1]
    directions = gains.shape[2]
    each = comps // directions
    orders = coef_tiles.shape[0] // 2
    width = coef_ref.shape[1]
    owners = block // width
    channels = local * sizes[2]
    devices = sizes[0] * sizes[1]
    every = ("row", "col", "freq")
    plane = lax.axis_index("row") * sizes[1] + lax.axis_index("col")
    here = {axis: lax.axis_index(axis) for axis in every}

    vis_copy = pltpu.make_async_copy(vis_hbm, vis_ref, vis_sem)
    vis_copy.start()
    barrier = pltpu.get_barrier_semaphore()

    def signal(j, where):
        pl.semaphore_signal(barrier, inc=1, device_id=where, device_id_type=MESH)

    walk(sizes, every, signal)

    for base, ref in ((0, coef_ref), (8, flag_ref)):
        tile = jnp.zeros((8, LANES), F32)
        for g in range(ref.shape[0] // 8):
            tile = tile + put_lanes(ref[8 * g : 8 * g + 8, :].astype(F32), g * width)
        all_ref[plane, base : base + 8, :] = tile

    def entry(n, shape):
        return jnp.broadcast_to(task_ref[0:1, n : n + 1], shape)

    def choose(n, pieces):
        total = jnp.zeros_like(pieces[0])
        for number, piece in enumerate(pieces):
            total = jnp.where(entry(n, piece.shape) == number, piece, total)
        return total


    drow = direction_ref[...].astype(F32)
    count = jnp.zeros((1, comps), F32)
    krow = lax.broadcasted_iota(jnp.int32, (LANES, comps), 1)
    jcol = lax.broadcasted_iota(jnp.int32, (LANES, comps), 0)
    for j in range(comps // LANES):
        piece = jnp.broadcast_to(drow[:, j * LANES : (j + 1) * LANES], (LANES, LANES))
        column = jnp.transpose(piece)
        column = jnp.concatenate([column] * (comps // LANES), axis=1)
        same = jnp.logical_and(column == drow, jcol + j * LANES < krow)
        count = count + jnp.sum(same.astype(F32), axis=0, keepdims=True)
    place = drow * each + count
    east, north = lm_ref[0:1, :], lm_ref[1:2, :]
    depth = jnp.sqrt(1.0 - east * east - north * north) - 1.0
    bright = intensity_ref[...]
    for d in range(directions):
        rows = pl.ds(d * each, each)
        found = (lax.broadcasted_iota(jnp.int32, (each, comps), 0) + d * each).astype(F32) == place
        for n, value in enumerate((east, north, depth, bright)):
            column = jnp.sum(jnp.where(found, value, 0.0), axis=1, keepdims=True)
            if n < 3:
                sky[n, rows, :] = jnp.broadcast_to(column, (each, LANES))
            else:
                wide = jnp.broadcast_to(column, (each, LANES))
                mixed = lax.broadcasted_iota(jnp.int32, (each, LANES), 1) < block
                paired = entry(2, (each, LANES)) == 2
                sky[3, rows, :] = jnp.where(paired, jnp.sqrt(wide), jnp.where(mixed, wide, 1.0))

    pl.semaphore_wait(barrier, math.prod(sizes) - 1)

    def send_gains(j, where):
        pltpu.make_async_remote_copy(
            src_ref=all_ref.at[plane],
            dst_ref=all_ref.at[plane],
            send_sem=gather_send,
            recv_sem=gather_recv,
            device_id=where,
            device_id_type=MESH,
        ).start()

    walk(sizes[:2], every[:2], send_gains)

    start = lax.axis_index("freq") * local
    points = [
        (2.0 * (start + f).astype(F32) - (channels - 1)) / (channels - 1) for f in range(local)
    ]
    factor = 1.0 + 0.15 * points[0]
    spacing = 0.15 * 2.0 / (channels - 1)

    def side_tile(n, task_entry, side):
        pieces = []
        for blk in range(uvw_ref.shape[2] // block):
            tile = uvw_ref[n, :, blk // 2 * LANES : (blk // 2 + 1) * LANES]
            pieces.append(tile if blk % 2 == side else halves_swapped(tile))
        return choose(task_entry, pieces)

    def by_time(a, b):
        kind = entry(2, (times, LANES))
        a = jnp.where(kind == 1, a[times:], a[:times])
        b = jnp.where(kind == 0, b[:times], b[times:])
        return jnp.where(lax.broadcasted_iota(jnp.int32, (times, LANES), 1) < block, a, b)

    for n in range(3):
        places[n] = by_time(side_tile(n, 0, 0), side_tile(n, 1, 1))

    def positions(t):
        return [places[n, pl.ds(t, 1), :] for n in range(3)]

    def turns_of(uvw, rows):
        return sky[0, rows, :] * uvw[0] + sky[1, rows, :] * uvw[1] + sky[2, rows, :] * uvw[2]

    def make_base(uvw, d):
        rows = pl.ds(d * each, each)
        c, s = turn_cos_sin(turns_of(uvw, rows) * factor)
        phase[0, 0, rows, :] = c * sky[3, rows, :]
        phase[0, 1, rows, :] = s * sky[3, rows, :]

    def make_step(uvw, d):
        rows = pl.ds(d * each, each)
        c, s = turn_cos_sin(turns_of(uvw, rows) * spacing)
        step_table[0, rows, :] = 2.0 * c
        step_table[1, rows, :] = s

    def make_x(f):
        for d in range(directions):
            rows = pl.ds(d * each, each)
            if f == 0:
                c, s = phase[0, 0, rows, :], phase[0, 1, rows, :]
            else:
                c1, s1 = phase[f - 1, 0, rows, :], phase[f - 1, 1, rows, :]
                twice = step_table[0, rows, :]
                if f == 1:
                    ec, es = 0.5 * twice, step_table[1, rows, :]
                    c = c1 * ec - s1 * es
                    s = s1 * ec + c1 * es
                else:
                    c = c1 * twice - phase[f - 2, 0, rows, :]
                    s = s1 * twice - phase[f - 2, 1, rows, :]
                phase[f, 0, rows, :] = c
                phase[f, 1, rows, :] = s
            gr, gi = gains[f, 0, d : d + 1, :], gains[f, 1, d : d + 1, :]
            x_ref[f, rows, 0:LANES] = (gr * c + gi * s).astype(jnp.bfloat16)
            x_ref[f, rows, LANES : 2 * LANES] = (gi * c - gr * s).astype(jnp.bfloat16)

    def make_z(f):
        x = x_ref[f]
        z_ref[f % 2] = lax.dot_general(
            x, x, (((0,), (0,)), ((), ())), preferred_element_type=F32
        )

    uvw = positions(0)
    for d in range(directions):
        make_base(uvw, d)
        make_step(uvw, d)
    sums[...] = jnp.zeros_like(sums)

    i = lax.broadcasted_iota(jnp.int32, (block, LANES), 0)
    j = lax.broadcasted_iota(jnp.int32, (block, LANES), 1)
    left = j < block
    j = jnp.where(left, j, j - block)
    upper = (i < j).astype(F32)
    lower = (i > j).astype(F32)
    leftf = left.astype(F32)
    paired = entry(2, (block, LANES)) == 2
    pick_a = jnp.where(paired, upper, 1.0)
    pick_b = jnp.where(paired, lower, 0.0)
    unequal = upper + lower
    mask_a = jnp.where(paired, unequal * leftf, 1.0 - leftf)
    mask_b = jnp.where(paired, unequal * (1.0 - leftf), leftf)

    others = all_ref.at[pl.ds(0, devices - 1)]
    gathered = pltpu.make_async_remote_copy(
        src_ref=others,
        dst_ref=others,
        send_sem=gather_send,
        recv_sem=gather_recv,
        device_id=here,
        device_id_type=MESH,
    )
    gathered.wait_send()
    gathered.wait_recv()

    flag_tiles = []
    sent = [
        [
            choose(side, [all_ref[blk * owners + i] for blk in range(devices // owners)])
            for i in range(owners)
        ]
        for side in range(2)
    ]
    for g in range(2 * orders + flag_ref.shape[0] // 8):
        base, at = (0, g) if g < 2 * orders else (8, g - 2 * orders)
        tile = jnp.zeros((8, LANES), F32)
        for side in range(2):
            for i in range(owners):
                piece = sent[side][i][base : base + 8, at * width : (at + 1) * width]
                tile = tile + put_lanes(piece, side * block + i * width)
        if g < 2 * orders:
            coef_tiles[g] = tile
        else:
            flag_tiles.append(tile)
    all_flags = jnp.concatenate(flag_tiles, axis=0)
    flags[...] = by_time(all_flags, all_flags)
    for f in range(local):
        for c in range(2):
            value = coef_tiles[2 * orders - 2 + c]
            for n in range(orders - 2, -1, -1):
                value = value * points[f] + coef_tiles[2 * n + c]
            gains[f, c] = value

    def make_weight(t, unused):
        good = jnp.broadcast_to(flags[pl.ds(t, 1), :], (LANES, LANES))
        both = good * jnp.transpose(good)
        weight[t, 0:block, :] = both[0:block] * mask_a
        weight[t, block : 2 * block, :] = both[block : 2 * block] * mask_b
        return unused

    lax.fori_loop(0, times, make_weight, 0)
    make_x(0)
    make_z(0)
    make_x(1)
    vis_copy.wait()

    def residual(t, f):
        v = vis_ref[t, f].astype(F32)
        turned = jnp.transpose(jnp.concatenate([v, v], axis=0))
        swapped = halves_swapped(v)
        real, imag = jnp.where(left, v, swapped), jnp.where(left, swapped, v)
        z = z_ref[f % 2]
        model_r = z[0:LANES, 0:LANES] + z[LANES:, LANES:]
        model_i = z[0:LANES, LANES:] - z[LANES:, 0:LANES]
        parts_r, parts_i = [], []
        for side, pick in ((0, pick_a), (1, pick_b)):
            rows = slice(side * block, (side + 1) * block)
            want = pick > 0.5
            vr = jnp.where(want, real, turned[0:block])
            vi = jnp.where(want, -imag, turned[block:])
            w = weight[t, rows, :]
            parts_r.append(w * (vr - model_r[rows]))
            parts_i.append(w * (vi - model_i[rows]))
        er = jnp.concatenate(parts_r, axis=0).astype(jnp.bfloat16)
        ei = jnp.concatenate(parts_i, axis=0).astype(jnp.bfloat16)
        return jnp.concatenate(
            [jnp.concatenate([er, ei], axis=1), jnp.concatenate([-ei, er], axis=1)], axis=0
        )

    def one_time(t, unused):
        later = positions(lax.rem(t + 1, times))
        spread = local >= 8
        for f in range(local):
            e = residual(t, f)
            h = jnp.dot(x_ref[f], e, preferred_element_type=F32)
            make_z((f + 1) % local)
            if f + 2 < local:
                make_x(f + 2)
            for d in range(directions):
                rows = slice(d * each, (d + 1) * each)
                c, s = phase[f, 0, rows, :], phase[f, 1, rows, :]
                hr, hi = h[rows, 0:LANES], h[rows, LANES:]
                tr = jnp.sum((c * hr - s * hi).reshape(each // 8, 8, LANES), axis=0)
                ti = jnp.sum((c * hi + s * hr).reshape(each // 8, 8, LANES), axis=0)
                sums[f, 0, d] += tr
                sums[f, 1, d] += ti
            for d in range(directions):
                if (f == 1 + d * (local - 3) // directions) if spread else f == local - 2:
                    make_base(later, d)
                if f == local - 2:
                    make_step(later, d)
            if f + 2 >= local:
                make_x(f + 2 - local)
        return unused

    lax.fori_loop(0, times, one_time, 0)

    scale = -1.0 / math.sqrt(2 * times * channels * devices * width)
    tiles = [None] * (2 * orders)
    for f in range(local):
        for c in range(2):
            total = jnp.sum(sums[f, c], axis=1) * scale
            for n in range(orders):
                old = tiles[2 * n + c]
                tiles[2 * n + c] = total if old is None else old + total
                total = total * points[f]
    for i in range(owners):
        packed = []
        for side in range(2):
            at = side * block + i * width
            pieces = [tiles[g][:, at : at + width] for g in range(2 * orders)]
            packed.append(put_lanes(jnp.concatenate(pieces, axis=1), 0))
        for blk in range(devices // owners):
            in_first = entry(0, packed[0].shape) == blk
            in_second = entry(1, packed[1].shape) == blk
            part_ref[blk * owners + i] = jnp.where(in_first, packed[0], 0.0) + jnp.where(
                in_second, packed[1], 0.0
            )

    def send_terms(j, where):
        pltpu.make_async_remote_copy(
            src_ref=part_ref.at[where["row"] * sizes[1] + where["col"]],
            dst_ref=held.at[j],
            send_sem=reduce_send,
            recv_sem=reduce_recv,
            device_id=where,
            device_id_type=MESH,
        ).start()

    walk(sizes, every, send_terms)
    arrived = pltpu.make_async_remote_copy(
        src_ref=held,
        dst_ref=held,
        send_sem=reduce_send,
        recv_sem=reduce_recv,
        device_id=here,
        device_id_type=MESH,
    )
    arrived.wait_recv()
    total = part_ref[plane] + jnp.sum(held[...], axis=0)
    for g in range(2 * orders):
        out_ref[8 * g : 8 * g + 8, :] = total[:, g * width : (g + 1) * width]
    arrived.wait_send()


def on_device(sizes, visibility, tasks, flags, station_uvw, comp_lm, intensity, direction, coefs):
    devices = sizes[0] * sizes[1]
    orders, unused, directions, width = coefs.shape
    unused, times, local, block, unused = visibility.shape
    comps = direction.shape[0]
    vmem = pl.BlockSpec(memory_space=pltpu.VMEM)
    out = pl.pallas_call(
        functools.partial(kernel, sizes),
        out_shape=jax.ShapeDtypeStruct((orders * 2 * directions, width), F32),
        in_specs=[
            vmem,
            vmem,
            vmem,
            pl.BlockSpec(memory_space=pl.ANY),
        ]
        + [vmem] * 4,
        out_specs=vmem,
        scratch_shapes=[
            pltpu.VMEM((devices, 16, LANES), F32),
            pltpu.VMEM((devices, directions, LANES), F32),
            pltpu.VMEM((devices * sizes[2] - 1, directions, LANES), F32),
            pltpu.VMEM((times, local, block, 2 * block), jnp.bfloat16),
            pltpu.VMEM((2 * orders, directions, LANES), F32),
            pltpu.VMEM((local, 2, directions, LANES), F32),
            pltpu.VMEM((times, LANES), F32),
            pltpu.VMEM((3, times, LANES), F32),
            pltpu.VMEM((4, comps, LANES), F32),
            pltpu.VMEM((times, LANES, LANES), F32),
            pltpu.VMEM((2, comps, LANES), F32),
            pltpu.VMEM((local, 2, comps, LANES), F32),
            pltpu.VMEM((local, comps, 2 * LANES), jnp.bfloat16),
            pltpu.VMEM((2, 2 * LANES, 2 * LANES), F32),
            pltpu.VMEM((local, 2, directions, 8, LANES), F32),
        ]
        + [pltpu.SemaphoreType.DMA] * 5,
        compiler_params=pltpu.CompilerParams(
            collective_id=0, has_side_effects=True, vmem_limit_bytes=40 * 1024 * 1024
        ),
        name="gain_gradient",
    )(
        tasks,
        coefs.reshape(orders * 2 * directions, width),
        flags,
        visibility[0],
        jnp.transpose(station_uvw, (1, 0, 2)),
        comp_lm,
        intensity.reshape(1, comps),
        direction.reshape(1, comps),
    )
    return out.reshape(orders, 2, directions, width)


def solution(mesh):
    sizes = tuple(mesh.shape[axis] for axis in ("row", "col", "freq"))
    return jax.shard_map(
        functools.partial(on_device, sizes),
        mesh=mesh,
        in_specs=(
            P(("row", "col"), None, "freq", None, None),
            P(("row", "col"), None),
            P(None, ("row", "col")),
            P(),
            P(),
            P(),
            P(),
            P(None, None, None, ("row", "col")),
        ),
        out_specs=P(None, None, None, ("row", "col")),
        check_vma=False,
    )
```

time: 54.7 us -> 48.7 us (0.89)
  Pallas kernels: 49.2 us -> 42.2 us
  local copies, waits for them, and re-layouts: 4.98 us -> 6.14 us
    pallas_call x3 -> x1, Pallas kernels: 49.2 us -> 42.2 us  [on_device(): pl.pallas_call(functools.partial(kernel, sizes), out_shape=jax.ShapeDtype...]
    unnamed x16 -> x17, local copies, waits for them, and re-layouts: 4.98 us -> 6.14 us
where the time goes in v2:
time: 48.7 us; the launch traced here: 48.4 us
  Pallas kernels  42.2 us (87%)
  local copies, waits for them, and re-layouts  6.14 us (13%)
    pallas_call x1, Pallas kernels, on_device(): pl.pallas_call(functools.partial(kernel, sizes), out_shape=jax.ShapeDtype...  42.2 us
    unnamed x17, local copies, waits for them, and re-layouts  6.14 us

profile of v2, /device:TPU:0, one launch (start us, length us, event | category | flops | bytes accessed | tf_op | source)
XLA Modules:
  0.0 48.4 jit_solution(6189846861147699925)
XLA Ops:
  0.0 0.0 copy-start.3
  0.0 0.0 copy-start.7
  0.0 0.7 %copy-done.3 = s32[16,16]{1,0:T(8,128)S(1)} copy-done((s32[16,16]{1,0:T(8,128)S(1)}, s32[16,16]{1,0:T(8,128)}, u32[]{:S(2)}) %copy-start.3) | copy-done | bytes 1048
  0.7 0.0 copy-done.7
  0.7 0.0 copy-start
  0.7 1.2 %copy-done = bf16[1,8,8,64,128]{4,3,2,1,0:T(8,128)(2,1)S(1)} copy-done((bf16[1,8,8,64,128]{4,3,2,1,0:T(8,128)(2,1)S(1)}, bf16[1,8,8,64,128]{4,3,2,1,0:T(8,128)(2,1)}, u32[]{:S(2)}) %copy-start) | copy-done | bytes 1048600
  1.9 0.0 copy-start.1
  1.9 0.8 %copy-done.1 = f32[16,3,256]{2,0,1:T(8,128)S(1)} copy-done((f32[16,3,256]{2,0,1:T(8,128)S(1)}, f32[16,3,256]{2,0,1:T(8,128)}, u32[]{:S(2)}) %copy-start.1) | copy-done | bytes 49176
  2.7 0.0 copy-start.2
  2.7 0.8 %copy-done.2 = f32[4,2,8,16]{3,2,1,0:T(8,128)S(1)} copy-done((f32[4,2,8,16]{3,2,1,0:T(8,128)S(1)}, f32[4,2,8,16]{3,2,1,0:T(8,128)}, u32[]{:S(2)}) %copy-start.2) | copy-done | bytes 4120
  3.5 0.0 copy-start.4
  3.5 0.7 %copy-done.4 = f32[2,512]{1,0:T(2,128)S(1)} copy-done((f32[2,512]{1,0:T(2,128)S(1)}, f32[2,512]{1,0:T(2,128)}, u32[]{:S(2)}) %copy-start.4) | copy-done | bytes 4120
  4.2 0.0 copy-start.5
  4.2 0.7 %copy-done.5 = f32[512]{0:T(512)S(1)} copy-done((f32[512]{0:T(512)S(1)}, f32[512]{0:T(512)}, u32[]{:S(2)}) %copy-start.5) | copy-done | bytes 2072
  4.9 0.0 copy-start.6
  4.9 0.7 %copy-done.6 = s32[512]{0:T(512)S(1)} copy-done((s32[512]{0:T(512)S(1)}, s32[512]{0:T(512)}, u32[]{:S(2)}) %copy-start.6) | copy-done | bytes 2072
  5.5 42.2 %gain_gradient.1 = f32[64,16]{1,0:T(8,128)S(1)} custom-call(s32[1,3]{1,0:T(1,128)S(1)} %copy-done.7, f32[64,16]{1,0:T(8,128)S(1)} %bitcast.9, s32[16,16]{1,0:T(8,128)S(1)} %copy-done.3, bf16[8,8,64,128]{3,2,1,0:T(8,128)(2,1)S(1)} %bitcast.6, f32[3,16,256]{2,1,0:T(8,128)S(1)} %bitcast.8, f32[2,512]{1,0:T(2,128)S(1)} %copy-done.4, f32[1,512]{1,0:T(1,128)S(1)} %bitcast.10, ...), custom_call_target="tpu_custom_call" | custom-call | tf_op jit(solution)/shard_map/gain_gradient/pallas_call | solution.py:442
  47.7 0.6 %copy.10 = f32[4,2,8,16]{3,2,1,0:T(8,128)} copy(f32[4,2,8,16]{3,2,1,0:T(8,128)S(1)} %bitcast.7) | data formatting | bytes 8192
Async XLA Ops:
  0.0 0.7 %copy-start.3 = (s32[16,16]{1,0:T(8,128)S(1)}, s32[16,16]{1,0:T(8,128)}, u32[]{:S(2)}) copy-start(s32[16,16]{1,0:T(8,128)} %flag_ref.1) | copy-start | bytes 3076
  0.0 0.7 %copy-start.7 = (s32[1,3]{1,0:T(1,128)S(1)}, s32[1,3]{1,0:T(1,128)}, u32[]{:S(2)}) copy-start(s32[1,3]{1,0:T(1,128)} %task_ref.1) | copy-start | bytes 40
  0.7 1.2 %copy-start = (bf16[1,8,8,64,128]{4,3,2,1,0:T(8,128)(2,1)S(1)}, bf16[1,8,8,64,128]{4,3,2,1,0:T(8,128)(2,1)}, u32[]{:S(2)}) copy-start(bf16[1,8,8,64,128]{4,3,2,1,0:T(8,128)(2,1)} %param.8) | copy-start | bytes 3145732
  1.9 0.8 %copy-start.1 = (f32[16,3,256]{2,0,1:T(8,128)S(1)}, f32[16,3,256]{2,0,1:T(8,128)}, u32[]{:S(2)}) copy-start(f32[16,3,256]{2,0,1:T(8,128)} %param.11) | copy-start | bytes 147460
  2.7 0.8 %copy-start.2 = (f32[4,2,8,16]{3,2,1,0:T(8,128)S(1)}, f32[4,2,8,16]{3,2,1,0:T(8,128)}, u32[]{:S(2)}) copy-start(f32[4,2,8,16]{3,2,1,0:T(8,128)} %param.15) | copy-start | bytes 12292
  3.5 0.7 %copy-start.4 = (f32[2,512]{1,0:T(2,128)S(1)}, f32[2,512]{1,0:T(2,128)}, u32[]{:S(2)}) copy-start(f32[2,512]{1,0:T(2,128)} %lm_ref.1) | copy-start | bytes 12292
  4.2 0.7 %copy-start.5 = (f32[512]{0:T(512)S(1)}, f32[512]{0:T(512)}, u32[]{:S(2)}) copy-start(f32[512]{0:T(512)} %param.13) | copy-start | bytes 6148
  4.9 0.7 %copy-start.6 = (s32[512]{0:T(512)S(1)}, s32[512]{0:T(512)}, u32[]{:S(2)}) copy-start(s32[512]{0:T(512)} %param.14) | copy-start | bytes 6148

commit v3 on v2

--- a/solution.py
+++ b/solution.py
@@ -22,7 +22,7 @@
 
 
 SIN_FIT = fit_even(lambda r: np.sin(np.pi * r) / r, 5)
-COS_FIT = fit_even(lambda r: np.cos(np.pi * r), 6)
+COS_FIT = fit_even(lambda r: np.cos(np.pi * r), 5)
 
 
 def horner(coefficients, z):
@@ -84,19 +84,28 @@
 
 def kernel(
     sizes,
+    task_hbm,
+    coef_hbm,
+    flag_hbm,
+    direction_hbm,
+    lm_hbm,
+    intensity_hbm,
+    uvw_hbm,
+    vis_hbm,
+    out_ref,
     task_ref,
     coef_ref,
     flag_ref,
-    vis_hbm,
-    uvw_ref,
+    direction_ref,
     lm_ref,
     intensity_ref,
-    direction_ref,
-    out_ref,
+    uvw_ref,
+    vis_ref,
     all_ref,
     part_ref,
     held,
-    vis_ref,
+    summed,
+    held_sums,
     coef_tiles,
     gains,
     flags,
@@ -104,6 +113,7 @@
     sky,
     weight,
     step_table,
+    turned_by,
     phase,
     x_ref,
     z_ref,
@@ -112,7 +122,9 @@
     gather_recv,
     reduce_send,
     reduce_recv,
-    vis_sem,
+    last_send,
+    last_recv,
+    load_sems,
 ):
     times, local, block = vis_ref.shape[0], vis_ref.shape[1], vis_ref.shape[2]
     comps = sky.shape[1]
@@ -127,14 +139,33 @@
     plane = lax.axis_index("row") * sizes[1] + lax.axis_index("col")
     here = {axis: lax.axis_index(axis) for axis in every}
 
-    vis_copy = pltpu.make_async_copy(vis_hbm, vis_ref, vis_sem)
-    vis_copy.start()
+    loads = [
+        pltpu.make_async_copy(source, target, load_sems.at[n])
+        for n, (source, target) in enumerate(
+            (
+                (coef_hbm, coef_ref),
+                (flag_hbm, flag_ref),
+                (direction_hbm, direction_ref),
+                (task_hbm, task_ref),
+                (lm_hbm, lm_ref),
+                (intensity_hbm, intensity_ref),
+                (uvw_hbm, uvw_ref),
+                (vis_hbm, vis_ref),
+            )
+        )
+    ]
+    for load in loads:
+        load.start()
     barrier = pltpu.get_barrier_semaphore()
 
     def signal(j, where):
         pl.semaphore_signal(barrier, inc=1, device_id=where, device_id_type=MESH)
 
-    walk(sizes, every, signal)
+    walk(sizes[:2], every[:2], signal)
+    walk(sizes[2:], every[2:], signal)
+
+    for load in loads[:-1]:
+        load.wait()
 
     for base, ref in ((0, coef_ref), (8, flag_ref)):
         tile = jnp.zeros((8, LANES), F32)
@@ -151,6 +182,12 @@
             total = jnp.where(entry(n, piece.shape) == number, piece, total)
         return total
 
+
+    start = lax.axis_index("freq") * local
+    points = [
+        (2.0 * (start + f).astype(F32) - (channels - 1)) / (channels - 1) for f in range(local)
+    ]
+    factor = 1.0 + 0.15 * points[0]
 
     drow = direction_ref[...].astype(F32)
     count = jnp.zeros((1, comps), F32)
@@ -172,14 +209,14 @@
         for n, value in enumerate((east, north, depth, bright)):
             column = jnp.sum(jnp.where(found, value, 0.0), axis=1, keepdims=True)
             if n < 3:
-                sky[n, rows, :] = jnp.broadcast_to(column, (each, LANES))
+                sky[n, rows, :] = jnp.broadcast_to(column * factor, (each, LANES))
             else:
                 wide = jnp.broadcast_to(column, (each, LANES))
                 mixed = lax.broadcasted_iota(jnp.int32, (each, LANES), 1) < block
                 paired = entry(2, (each, LANES)) == 2
                 sky[3, rows, :] = jnp.where(paired, jnp.sqrt(wide), jnp.where(mixed, wide, 1.0))
 
-    pl.semaphore_wait(barrier, math.prod(sizes) - 1)
+    pl.semaphore_wait(barrier, devices - 1 + sizes[2] - 1)
 
     def send_gains(j, where):
         pltpu.make_async_remote_copy(
@@ -193,12 +230,7 @@
 
     walk(sizes[:2], every[:2], send_gains)
 
-    start = lax.axis_index("freq") * local
-    points = [
-        (2.0 * (start + f).astype(F32) - (channels - 1)) / (channels - 1) for f in range(local)
-    ]
-    factor = 1.0 + 0.15 * points[0]
-    spacing = 0.15 * 2.0 / (channels - 1)
+    spacing = 0.15 * 2.0 / (channels - 1) / factor
 
     def side_tile(n, task_entry, side):
         pieces = []
@@ -224,13 +256,15 @@
 
     def make_base(uvw, d):
         rows = pl.ds(d * each, each)
-        c, s = turn_cos_sin(turns_of(uvw, rows) * factor)
+        turns = turns_of(uvw, rows)
+        turned_by[rows, :] = turns
+        c, s = turn_cos_sin(turns)
         phase[0, 0, rows, :] = c * sky[3, rows, :]
         phase[0, 1, rows, :] = s * sky[3, rows, :]
 
-    def make_step(uvw, d):
+    def make_step(d):
         rows = pl.ds(d * each, each)
-        c, s = turn_cos_sin(turns_of(uvw, rows) * spacing)
+        c, s = turn_cos_sin(turned_by[rows, :] * spacing)
         step_table[0, rows, :] = 2.0 * c
         step_table[1, rows, :] = s
 
@@ -264,7 +298,7 @@
     uvw = positions(0)
     for d in range(directions):
         make_base(uvw, d)
-        make_step(uvw, d)
+        make_step(d)
     sums[...] = jnp.zeros_like(sums)
 
     i = lax.broadcasted_iota(jnp.int32, (block, LANES), 0)
@@ -332,7 +366,7 @@
     make_x(0)
     make_z(0)
     make_x(1)
-    vis_copy.wait()
+    loads[-1].wait()
 
     def residual(t, f):
         v = vis_ref[t, f].astype(F32)
@@ -378,7 +412,7 @@
                 if (f == 1 + d * (local - 3) // directions) if spread else f == local - 2:
                     make_base(later, d)
                 if f == local - 2:
-                    make_step(later, d)
+                    make_step(d)
             if f + 2 >= local:
                 make_x(f + 2 - local)
         return unused
@@ -417,7 +451,7 @@
             device_id_type=MESH,
         ).start()
 
-    walk(sizes, every, send_terms)
+    walk(sizes[:2], every[:2], send_terms)
     arrived = pltpu.make_async_remote_copy(
         src_ref=held,
         dst_ref=held,
@@ -427,9 +461,32 @@
         device_id_type=MESH,
     )
     arrived.wait_recv()
-    total = part_ref[plane] + jnp.sum(held[...], axis=0)
+    summed[...] = part_ref[plane] + jnp.sum(held[...], axis=0)
+
+    def send_sum(j, where):
+        pltpu.make_async_remote_copy(
+            src_ref=summed,
+            dst_ref=held_sums.at[j],
+            send_sem=last_send,
+            recv_sem=last_recv,
+            device_id=where,
+            device_id_type=MESH,
+        ).start()
+
+    walk(sizes[2:], every[2:], send_sum)
+    last = pltpu.make_async_remote_copy(
+        src_ref=held_sums,
+        dst_ref=held_sums,
+        send_sem=last_send,
+        recv_sem=last_recv,
+        device_id=here,
+        device_id_type=MESH,
+    )
+    last.wait_recv()
+    total = summed[...] + jnp.sum(held_sums[...], axis=0)
     for g in range(2 * orders):
         out_ref[8 * g : 8 * g + 8, :] = total[:, g * width : (g + 1) * width]
+    last.wait_send()
     arrived.wait_send()
 
 
@@ -438,23 +495,28 @@
     orders, unused, directions, width = coefs.shape
     unused, times, local, block, unused = visibility.shape
     comps = direction.shape[0]
-    vmem = pl.BlockSpec(memory_space=pltpu.VMEM)
+    inputs = (
+        tasks,
+        coefs.reshape(orders * 2 * directions, width),
+        flags,
+        direction.reshape(1, comps),
+        comp_lm,
+        intensity.reshape(1, comps),
+        jnp.transpose(station_uvw, (1, 0, 2)),
+        visibility[0],
+    )
     out = pl.pallas_call(
         functools.partial(kernel, sizes),
         out_shape=jax.ShapeDtypeStruct((orders * 2 * directions, width), F32),
-        in_specs=[
-            vmem,
-            vmem,
-            vmem,
-            pl.BlockSpec(memory_space=pl.ANY),
-        ]
-        + [vmem] * 4,
-        out_specs=vmem,
-        scratch_shapes=[
+        in_specs=[pl.BlockSpec(memory_space=pltpu.HBM)] * len(inputs),
+        out_specs=pl.BlockSpec(memory_space=pltpu.VMEM),
+        scratch_shapes=[pltpu.VMEM(value.shape, value.dtype) for value in inputs]
+        + [
             pltpu.VMEM((devices, 16, LANES), F32),
             pltpu.VMEM((devices, directions, LANES), F32),
-            pltpu.VMEM((devices * sizes[2] - 1, directions, LANES), F32),
-            pltpu.VMEM((times, local, block, 2 * block), jnp.bfloat16),
+            pltpu.VMEM((devices - 1, directions, LANES), F32),
+            pltpu.VMEM((directions, LANES), F32),
+            pltpu.VMEM((sizes[2] - 1, directions, LANES), F32),
             pltpu.VMEM((2 * orders, directions, LANES), F32),
             pltpu.VMEM((local, 2, directions, LANES), F32),
             pltpu.VMEM((times, LANES), F32),
@@ -462,26 +524,19 @@
             pltpu.VMEM((4, comps, LANES), F32),
             pltpu.VMEM((times, LANES, LANES), F32),
             pltpu.VMEM((2, comps, LANES), F32),
+            pltpu.VMEM((comps, LANES), F32),
             pltpu.VMEM((local, 2, comps, LANES), F32),
             pltpu.VMEM((local, comps, 2 * LANES), jnp.bfloat16),
             pltpu.VMEM((2, 2 * LANES, 2 * LANES), F32),
             pltpu.VMEM((local, 2, directions, 8, LANES), F32),
         ]
-        + [pltpu.SemaphoreType.DMA] * 5,
+        + [pltpu.SemaphoreType.DMA] * 6
+        + [pltpu.SemaphoreType.DMA((len(inputs),))],
         compiler_params=pltpu.CompilerParams(
-            collective_id=0, has_side_effects=True, vmem_limit_bytes=40 * 1024 * 1024
+            collective_id=0, has_side_effects=True, vmem_limit_bytes=60 * 1024 * 1024
         ),
         name="gain_gradient",
-    )(
-        tasks,
-        coefs.reshape(orders * 2 * directions, width),
-        flags,
-        visibility[0],
-        jnp.transpose(station_uvw, (1, 0, 2)),
-        comp_lm,
-        intensity.reshape(1, comps),
-        direction.reshape(1, comps),
-    )
+    )(*inputs)
     return out.reshape(orders, 2, directions, width)
 
 

time: 48.7 us -> 43.7 us (0.90)
  local copies, waits for them, and re-layouts: 6.14 us -> 1.38 us
    unnamed x17 -> x1, local copies, waits for them, and re-layouts: 6.14 us -> 1.38 us
where the time goes in v3:
time: 43.7 us; the launch traced here: 43.5 us
  Pallas kernels  42.1 us (96%)
  local copies, waits for them, and re-layouts  1.38 us (3%)
    pallas_call x1, Pallas kernels, on_device(): pl.pallas_call(functools.partial(kernel, sizes), out_shape=jax.ShapeDtype...  42.1 us
    unnamed x1, local copies, waits for them, and re-layouts  1.38 us

profile of v3, /device:TPU:0, one launch (start us, length us, event | category | flops | bytes accessed | tf_op | source)
XLA Modules:
  0.0 43.5 jit_solution(12614157321430909167)
XLA Ops:
  0.0 42.1 %gain_gradient.1 = f32[64,16]{1,0:T(8,128)} custom-call(s32[1,3]{1,0:T(1,128)} %task_hbm.1, f32[64,16]{1,0:T(8,128)} %bitcast.9, s32[16,16]{1,0:T(8,128)} %flag_hbm.1, s32[1,512]{1,0:T(1,128)} %bitcast.10, f32[2,512]{1,0:T(2,128)} %lm_hbm.1, f32[1,512]{1,0:T(1,128)} %bitcast.11, f32[3,16,256]{2,1,0:T(8,128)} %bitcast.8, bf16[8,8,64,128]{3,2,1,0:T(8,128)(2,1)} %bitcast.6), custom_call_target="tpu_custom_call" | custom-call | tf_op jit(solution)/shard_map/gain_gradient/pallas_call | solution.py:508
  42.1 1.4 %copy.10 = f32[4,2,8,16]{3,2,1,0:T(8,128)} copy(f32[4,2,8,16]{3,2,1,0:T(8,128)} %bitcast.7) | data formatting | bytes 8192
